TPU v7x, 32 devices: a whole 2x2x4 slice. The times are simulated.
32 devices in a mesh: dp: 16 (over z, y, x), mp: 2 (over core).
Axes of the slice: x: 2, y: 2, z: 4, core: 2. Of those that a mesh axis runs over, the one named last changes fastest.
Arguments:
- tokens: bfloat16 [65536, 512], P(('dp', 'mp')), may hold values from -6 to 6
- segment_ids: int32 [128, 512], P('dp'), may hold values from 0 to 7, never falling along the last dimension, each value on 1 to 256 neighbouring positions
- cotangent: bfloat16 [65536, 512], P(('dp', 'mp')), may hold values from -6 to 6
- pos_table: bfloat16 [512, 512], replicated, may hold values from -3 to 3
- w_qkv: bfloat16 [512, 1536], P(None, 'mp'), may hold values from -0.25 to 0.25
- w_out: bfloat16 [512, 512], P('mp'), may hold values from -1 to 1
- w_up: bfloat16 [512, 2048], P(None, 'mp'), may hold values from -0.25 to 0.25
- w_down: bfloat16 [2048, 512], P('mp'), may hold values from -0.125 to 0.125
- gain_one: float32 [512], replicated, may hold values from 0.5 to 1.5
- bias_one: float32 [512], replicated, may hold values from -1 to 1
- gain_two: float32 [512], replicated, may hold values from 0.5 to 1.5
- bias_two: float32 [512], replicated, may hold values from -1 to 1
Outputs:
- output: bfloat16 [65536, 512], P(('dp', 'mp'))
- input_grad: bfloat16 [65536, 512], P(('dp', 'mp'))
- pos_grad: float32 [512, 512], replicated
- qkv_grad: float32 [512, 1536], P(None, 'mp')
- out_grad: float32 [512, 512], P('mp')
- up_grad: float32 [512, 2048], P(None, 'mp')
- down_grad: float32 [2048, 512], P('mp')
- gain_one_grad: float32 [512], replicated
- bias_one_grad: float32 [512], replicated
- gain_two_grad: float32 [512], replicated
- bias_two_grad: float32 [512], replicated
Inputs may be any that keep to these rules, and one draw needn't show every extreme that they name: `segment_ids`: within each window the numbers never fall, and each number covers 1 to 256 consecutive characters.
All inputs are finite; a program needn't handle non-finite values.
Results may differ from a plain program's by a relative error of at most 0.017.
Values may be sent and summed in bfloat16 or wider, within the bound.
A program may use at most 192 MiB of HBM per device.

v0:
```python
import jax
import jax.numpy as jnp
from jax import lax
from jax.sharding import PartitionSpec as P

HD = 64


EPSILON = 1e-05


def cross_rows(left_side, right_side):
    return lax.dot_general(
        left_side, right_side, (((0,), (0,)), ((), ())), preferred_element_type=jnp.float32
    )


def times_transposed(left_side, right_side):
    return lax.dot_general(
        left_side, right_side, (((1,), (1,)), ((), ())), preferred_element_type=jnp.float32
    )


def normalize(residual, gain_row, offset_row):
    center = residual - jnp.mean(residual, axis=-1, keepdims=True)
    scaled = lax.rsqrt(jnp.mean(center * center, axis=-1, keepdims=True) + EPSILON)
    normed = center * scaled
    return (normed * gain_row + offset_row, normed, scaled)


def normalize_back(upstream, normed, scaled, gain_row):
    weighted = upstream * gain_row
    return scaled * (
        weighted
        - jnp.mean(weighted, axis=-1, keepdims=True)
        - normed * jnp.mean(weighted * normed, axis=-1, keepdims=True)
    )


def allowed_mask(segment):
    places = jnp.arange(segment.shape[0])
    return (segment[:, None] == segment[None, :]) & (places[None, :] <= places[:, None])


def scores_of(queries, keys_in, segment):
    factor = HD ** (-0.5)
    scores = (
        jnp.einsum("qhd,khd->hqk", queries, keys_in, preferred_element_type=jnp.float32) * factor
    )
    return jnp.where(allowed_mask(segment)[None], scores, -1e30)


def attend(operands):
    joined_rows, segment = operands
    length = joined_rows.shape[0]
    shaped = joined_rows.reshape(length, -1, 3, HD)
    scores = scores_of(shaped[:, :, 0], shaped[:, :, 1], segment)
    highest = jnp.max(scores, axis=-1, keepdims=True)
    weights = jnp.exp(scores - highest)
    totals = jnp.sum(weights, axis=-1, keepdims=True)
    probabilities = (weights / totals).astype(jnp.bfloat16)
    mixture = jnp.einsum(
        "hqk,khd->qhd", probabilities, shaped[:, :, 2], preferred_element_type=jnp.float32
    )
    return (mixture.reshape(length, -1).astype(jnp.bfloat16), (highest + jnp.log(totals))[:, :, 0])


def attend_back(operands):
    joined_rows, mix_grad, log_total, segment = operands
    length = joined_rows.shape[0]
    shaped = joined_rows.reshape(length, -1, 3, HD)
    queries, keys_in, values = (shaped[:, :, 0], shaped[:, :, 1], shaped[:, :, 2])
    scores = scores_of(queries, keys_in, segment)
    probabilities = jnp.exp(scores - log_total[:, :, None])
    upstream = mix_grad.reshape(length, -1, HD)
    prob_grad = jnp.einsum("qhd,khd->hqk", upstream, values, preferred_element_type=jnp.float32)
    centre = jnp.sum(probabilities * prob_grad, axis=-1, keepdims=True)
    score_grad = (probabilities * (prob_grad - centre)).astype(jnp.bfloat16)
    factor = HD ** (-0.5)
    query_grad = (
        jnp.einsum("hqk,khd->qhd", score_grad, keys_in, preferred_element_type=jnp.float32) * factor
    )
    key_grad = (
        jnp.einsum("hqk,qhd->khd", score_grad, queries, preferred_element_type=jnp.float32) * factor
    )
    value_grad = jnp.einsum(
        "hqk,qhd->khd",
        probabilities.astype(jnp.bfloat16),
        upstream,
        preferred_element_type=jnp.float32,
    )
    stacked = jnp.stack((query_grad, key_grad, value_grad), axis=2)
    return stacked.reshape(length, -1).astype(jnp.bfloat16)


def local(
    tokens,
    segment_ids,
    cotangent,
    pos_table,
    w_qkv,
    w_out,
    w_up,
    w_down,
    gain_one,
    bias_one,
    gain_two,
    bias_two,
):
    shard_rows, model_width = tokens.shape
    window_len = pos_table.shape[0]
    placed = (
        tokens.astype(jnp.float32).reshape(-1, window_len, model_width)
        + pos_table.astype(jnp.float32)
    ).reshape(shard_rows, model_width)
    mixed_in = placed.astype(jnp.bfloat16)
    shard_piece = lax.all_gather(mixed_in, "mp", axis=0, tiled=True)
    joined_piece = jnp.dot(shard_piece, w_qkv, preferred_element_type=jnp.float32).astype(
        jnp.bfloat16
    )
    group_rows = joined_piece.shape[0]
    window_count = group_rows // window_len
    mixture, log_total = lax.map(
        attend, (joined_piece.reshape(window_count, window_len, -1), segment_ids)
    )
    mixture = mixture.reshape(group_rows, -1)
    attention = lax.psum_scatter(
        jnp.dot(mixture, w_out, preferred_element_type=jnp.float32).astype(jnp.bfloat16),
        "mp",
        scatter_dimension=0,
        tiled=True,
    ).astype(jnp.float32)
    normed_one, unit_one, scale_one = normalize(placed + attention, gain_one, bias_one)
    ffn_in = normed_one.astype(jnp.bfloat16)
    expand_shard_piece = lax.all_gather(ffn_in, "mp", axis=0, tiled=True)
    before_piece = jnp.dot(expand_shard_piece, w_up, preferred_element_type=jnp.float32)
    active_piece = jax.nn.gelu(before_piece).astype(jnp.bfloat16)
    ffn_out = lax.psum_scatter(
        jnp.dot(active_piece, w_down, preferred_element_type=jnp.float32).astype(jnp.bfloat16),
        "mp",
        scatter_dimension=0,
        tiled=True,
    ).astype(jnp.float32)
    normed_two, unit_two, scale_two = normalize(normed_one + ffn_out, gain_two, bias_two)
    output = normed_two.astype(jnp.bfloat16)
    upstream = cotangent.astype(jnp.float32)
    gain_two_grad = jnp.sum(upstream * unit_two, axis=0)
    bias_two_grad = jnp.sum(upstream, axis=0)
    resid_two_grad = normalize_back(upstream, unit_two, scale_two, gain_two)
    ffn_grad = resid_two_grad.astype(jnp.bfloat16)
    ffn_shard_piece = lax.all_gather(ffn_grad, "mp", axis=0, tiled=True)
    down_total = cross_rows(active_piece, ffn_shard_piece)
    active_grad = times_transposed(ffn_shard_piece, w_down)
    slope_grad = jax.vjp(jax.nn.gelu, before_piece)[1](active_grad)[0]
    ffn_before_grads = slope_grad.astype(jnp.bfloat16)
    down_grad = down_total
    normed_grad = resid_two_grad + lax.psum_scatter(
        times_transposed(ffn_before_grads, w_up).astype(jnp.bfloat16),
        "mp",
        scatter_dimension=0,
        tiled=True,
    ).astype(jnp.float32)
    up_grad = cross_rows(expand_shard_piece, ffn_before_grads)
    gain_one_grad = jnp.sum(normed_grad * unit_one, axis=0)
    bias_one_grad = jnp.sum(normed_grad, axis=0)
    resid_one_grad = normalize_back(normed_grad, unit_one, scale_one, gain_one)
    attn_grad = resid_one_grad.astype(jnp.bfloat16)
    attn_shard_piece = lax.all_gather(attn_grad, "mp", axis=0, tiled=True)
    out_total = cross_rows(mixture, attn_shard_piece)
    mix_rows = times_transposed(attn_shard_piece, w_out).astype(jnp.bfloat16)
    out_grad = out_total
    joined_grad = lax.map(
        attend_back,
        (
            joined_piece.reshape(window_count, window_len, -1),
            mix_rows.reshape(window_count, window_len, -1),
            log_total,
            segment_ids,
        ),
    )
    joined_grad = joined_grad.reshape(group_rows, -1)
    placed_grad = resid_one_grad + lax.psum_scatter(
        times_transposed(joined_grad, w_qkv).astype(jnp.bfloat16),
        "mp",
        scatter_dimension=0,
        tiled=True,
    ).astype(jnp.float32)
    qkv_grad = cross_rows(shard_piece, joined_grad)
    input_grad = placed_grad.astype(jnp.bfloat16)
    pos_grad = jnp.sum(placed_grad.reshape(-1, window_len, model_width), axis=0)
    qkv_grad, out_grad, up_grad, down_grad = lax.psum(
        (qkv_grad, out_grad, up_grad, down_grad), "dp"
    )
    pos_grad, gain_one_grad, bias_one_grad, gain_two_grad, bias_two_grad = lax.psum(
        (pos_grad, gain_one_grad, bias_one_grad, gain_two_grad, bias_two_grad), ("dp", "mp")
    )
    return (
        output,
        input_grad,
        pos_grad,
        qkv_grad,
        out_grad,
        up_grad,
        down_grad,
        gain_one_grad,
        bias_one_grad,
        gain_two_grad,
        bias_two_grad,
    )


def solution(mesh):
    in_specs = (
        P(("dp", "mp"), None),
        P("dp", None),
        P(("dp", "mp"), None),
        P(),
        P(None, "mp"),
        P("mp", None),
        P(None, "mp"),
        P("mp", None),
        P(),
        P(),
        P(),
        P(),
    )
    out_specs = (
        P(("dp", "mp"), None),
        P(("dp", "mp"), None),
        P(),
        P(None, "mp"),
        P("mp", None),
        P(None, "mp"),
        P("mp", None),
        P(),
        P(),
        P(),
        P(),
    )
    return jax.shard_map(local, mesh=mesh, in_specs=in_specs, out_specs=out_specs, check_vma=False)
```

profile of v0, /device:TPU:1, one launch (start us, length us, event | category | flops | bytes accessed | tf_op | source)
XLA Modules:
  0.0 788.6 jit_solution(2157114172756551198)
XLA Ops:
  13.2 16.2 %all-gather.5.cloned.1.call-done = bf16[4096,512]{1,0:T(8,128)(2,1)} async-done(((bf16[2048,512]{1,0:T(8,128)(2,1)}), bf16[4096,512]{1,0:T(8,128)(2,1)}) %all-gather.5.cloned.1.call-update) | async-done | bytes 4194320 | tf_op jit(solution)/shard_map/all_gather | solution.py:117
  29.4 8.3 %convolution_convert_fusion = bf16[4096,768]{1,0:T(8,128)(2,1)} fusion(bf16[4096,512]{1,0:T(8,128)(2,1)} %all-gather.5.cloned.1.call-done, bf16[512,768]{1,0:T(8,128)(2,1)S(1)} %copy-done.27), kind=kOutput, calls=%fused_computation.58 | convolution fusion | flops 3224371200 | bytes 11272192 | tf_op jit(solution)/shard_map/dot_general | solution.py:118
  37.7 8.6 %copy.54 = bf16[8,512,768]{1,2,0:T(8,128)(2,1)} copy(bf16[8,512,768]{2,1,0:T(8,128)(2,1)} %bitcast.179) | data formatting | bytes 12582912 | tf_op jit(solution)/shard_map/while | solution.py:123
  46.3 49.8 %while.22 = (s32[]{:T(128)}, bf16[8,512,256]{2,1,0:T(8,128)(2,1)}, f32[8,4,512]{2,1,0:T(4,128)S(1)}, bf16[8,512,768]{1,2,0:T(8,128)(2,1)}, s32[8,512]{1,0:T(8,128)}, /*index=5*/s32[]{:T(128)}) while((s32[]{:T(128)}, bf16[8,512,256]{2,1,0:T(8,128)(2,1)}, f32[8,4,512]{2,1,0:T(4,128)S(1)}, bf16[8,512,768]{1,2,0:T(8,128)(2,1)}, ...), condition=%wide.region_3.4_spmd, body=%wide.region_0.3_spmd.sunk | while | flops 281933824 | bytes 17373776 | solution.py:123
  96.1 4.9 convolution_convert_fusion.4
  101.5 12.9 %reduce-scatter.5.cloned.1.call-done = bf16[2048,512]{1,0:T(8,128)(2,1)} async-done(((bf16[4096,512]{1,0:T(8,128)(2,1)}), bf16[2048,512]{1,0:T(8,128)(2,1)}) %reduce-scatter.5.cloned.1.call-update) | async-done | bytes 2097168 | tf_op jit(solution)/shard_map/reduce_scatter | solution.py:127
  120.8 14.9 %all-gather.7.cloned.1.call-done = bf16[4096,512]{1,0:T(8,128)(2,1)} async-done(((bf16[2048,512]{1,0:T(8,128)(2,1)}), bf16[4096,512]{1,0:T(8,128)(2,1)}) %all-gather.7.cloned.1.call-update) | async-done | bytes 4194320 | tf_op jit(solution)/shard_map/all_gather | solution.py:135
  135.8 13.7 %multiply_convert_fusion.1 = (bf16[4096,1024]{1,0:T(8,128)(2,1)S(1)}, f32[4096,1024]{1,0:T(8,128)}) fusion(bf16[4096,512]{1,0:T(8,128)(2,1)} %all-gather.7.cloned.1.call-done, bf16[512,1024]{1,0:T(8,128)(2,1)S(1)} %copy-done), kind=kOutput, calls=%fused_computation.57 | convolution fusion | flops 4332716032 | bytes 30408704 | tf_op jit(solution)/shard_map/dot_general | solution.py:136
  152.7 6.0 convolution_convert_fusion.3
  159.0 13.3 %reduce-scatter.7.cloned.1.call-done = bf16[2048,512]{1,0:T(8,128)(2,1)} async-done(((bf16[4096,512]{1,0:T(8,128)(2,1)}), bf16[2048,512]{1,0:T(8,128)(2,1)}) %reduce-scatter.7.cloned.1.call-update) | async-done | bytes 2097168 | tf_op jit(solution)/shard_map/reduce_scatter | solution.py:138
  180.4 4.3 fusion.47
  184.7 14.9 %all-gather.9.cloned.1.call-done = bf16[4096,512]{1,0:T(8,128)(2,1)} async-done(((bf16[2048,512]{1,0:T(8,128)(2,1)}), bf16[4096,512]{1,0:T(8,128)(2,1)}) %all-gather.9.cloned.1.call-update) | async-done | bytes 4194320 | tf_op jit(solution)/shard_map/all_gather | solution.py:151
  199.7 16.9 %fusion.33 = bf16[4096,1024]{1,0:T(8,128)(2,1)S(1)} fusion(f32[4096,1024]{1,0:T(8,128)} %get-tuple-element.154, bf16[4096,512]{1,0:T(8,128)(2,1)} %all-gather.9.cloned.1.call-done, bf16[1024,512]{1,0:T(8,128)(2,1)} %param.23), kind=kOutput, calls=%fused_computation.56 | convolution fusion | flops 4378853376 | bytes 30408704 | tf_op jit(solution)/shard_map/dot_general | solution.py:19
  219.9 6.2 convolution_convert_fusion.2
  226.4 13.2 %reduce-scatter.9.cloned.1.call-done = bf16[2048,512]{1,0:T(8,128)(2,1)} async-done(((bf16[4096,512]{1,0:T(8,128)(2,1)}), bf16[2048,512]{1,0:T(8,128)(2,1)}) %reduce-scatter.9.cloned.1.call-update) | async-done | bytes 2097168 | tf_op jit(solution)/shard_map/reduce_scatter | solution.py:157
  239.6 5.7 multiply_reduce_fusion.1
  245.5 4.0 fusion.46
  249.6 15.0 %all-gather.11.cloned.1.call-done = bf16[4096,512]{1,0:T(8,128)(2,1)} async-done(((bf16[2048,512]{1,0:T(8,128)(2,1)}), bf16[4096,512]{1,0:T(8,128)(2,1)}) %all-gather.11.cloned.1.call-update) | async-done | bytes 4194320 | tf_op jit(solution)/shard_map/all_gather | solution.py:168
  264.6 4.8 convolution_convert_fusion.5
  269.4 120.9 %while.23 = (s32[]{:T(128)}, bf16[8,512,768]{2,1,0:T(8,128)(2,1)}, bf16[8,512,768]{1,2,0:T(8,128)(2,1)}, s32[8,512]{1,0:T(8,128)}, f32[8,4,512]{2,1,0:T(4,128)S(1)}, /*index=5*/bf16[8,512,256]{2,1,0:T(8,128)(2,1)}, s32[]{:T(128)}) while((s32[]{:T(128)}, bf16[8,512,768]{2,1,0:T(8,128)(2,1)}, bf16[8,512,768]{1,2,0:T(8,128)(2,1)}, ...), condition=%wide.region_17.18_spmd, body=%wide.region_15.17_spmd.sunk | while | flops 689043456 | bytes 60881528 | solution.py:172
  275.5 3.9 multiply_reduce_fusion.7
  351.1 3.9 multiply_reduce_fusion.7
  381.3 3.9 multiply_reduce_fusion.7
  390.3 7.8 convolution_convert_fusion.1
  398.5 10.6 %fusion.52 = f32[512,1024]{1,0:T(8,128)} fusion(bf16[4096,512]{1,0:T(8,128)(2,1)} %all-gather.7.cloned.1.call-done, bf16[4096,1024]{1,0:T(8,128)(2,1)} %copy-done.30), kind=kOutput, calls=%fused_computation.107 | convolution fusion | flops 4294967296 | bytes 14680064 | tf_op jit(solution)/shard_map/dot_general | solution.py:13
  409.1 8.7 %fusion.53 = f32[1024,512]{1,0:T(8,128)} fusion(bf16[4096,1024]{1,0:T(8,128)(2,1)} %copy-done.29, bf16[4096,512]{1,0:T(8,128)(2,1)S(1)} %copy-done.24), kind=kOutput, calls=%fused_computation.108 | convolution fusion | flops 4294967296 | bytes 14680064 | tf_op jit(solution)/shard_map/dot_general | solution.py:13
  420.0 4.6 fusion.50
  424.7 6.4 fusion.45
  431.1 4.3 reduce_sum.143
  435.4 43.2 %all-reduce = (f32[512]{0:T(512)}, f32[512]{0:T(512)}, f32[512]{0:T(512)}, f32[512]{0:T(512)}) all-reduce(f32[512]{0:T(512)S(1)} %get-tuple-element.102, f32[512]{0:T(512)S(1)} %get-tuple-element.107, f32[512]{0:T(512)S(1)} %copy-done.19, f32[512]{0:T(512)S(1)} %copy-done.20), channel_id=1, replica_groups=mesh['dp'=16,'mp'=2] {'dp','mp'}, use_global_device_ids=true, to_apply=%region_26.27 | all-reduce | flops 2048 | bytes 16384 | tf_op jit(solution)/shard_map/psum | solution.py:194
  478.6 159.7 %all-reduce.7.cloned.1.call-done = (f32[512,768]{1,0:T(8,128)}, f32[256,512]{1,0:T(8,128)}, f32[512,1024]{1,0:T(8,128)}, f32[1024,512]{1,0:T(8,128)}) async-done(((f32[512,768]{1,0:T(8,128)}, f32[256,512]{1,0:T(8,128)}, f32[512,1024]{1,0:T(8,128)}, f32[1024,512]{1,0:T(8,128)}), (f32[512,768]{1,0:T(8,128)}, f32[256,512]{1,0:T(8,128)}, f32[512,1024]{1,0:T(8,128)}, ...) | async-done | bytes 6291472 | tf_op jit(solution)/shard_map/psum | solution.py:191
  638.3 134.4 %all-reduce.5.cloned.1.call-done = f32[512,512]{1,0:T(8,128)} async-done(((f32[512,512]{1,0:T(8,128)}), f32[512,512]{1,0:T(8,128)}) %all-reduce.5.cloned.1.call-update) | async-done | bytes 1048592 | tf_op jit(solution)/shard_map/psum | solution.py:194
  (323 shorter events, 197.6 us)
Async XLA Ops:
  7.2 128.6 %copy-start = (bf16[512,1024]{1,0:T(8,128)(2,1)S(1)}, bf16[512,1024]{1,0:T(8,128)(2,1)}, u32[]{:S(2)}) copy-start(bf16[512,1024]{1,0:T(8,128)(2,1)} %param.22) | copy-start | bytes 3145732
  7.2 22.2 %copy-start.27 = (bf16[512,768]{1,0:T(8,128)(2,1)S(1)}, bf16[512,768]{1,0:T(8,128)(2,1)}, u32[]{:S(2)}) copy-start(bf16[512,768]{1,0:T(8,128)(2,1)} %param.20) | copy-start | bytes 2359300
  7.2 22.2 %all-gather.5.cloned.1.call-start = ((), (), s32[]{:S(2)}) async-start(), calls=%async_computation.4 | async-start | bytes 6291456 | tf_op jit(solution)/shard_map/all_gather | solution.py:117
  13.1 101.4 %reduce-scatter.5.cloned.1.call-start = ((), (), s32[]{:S(2)}) async-start(), calls=%async_computation.5 | async-start | bytes 6291456 | tf_op jit(solution)/shard_map/reduce_scatter | solution.py:127
  46.3 49.8 %copy-start.16 = (bf16[256,512]{1,0:T(8,128)(2,1)S(1)}, bf16[256,512]{1,0:T(8,128)(2,1)}, u32[]{:S(2)}) copy-start(bf16[256,512]{1,0:T(8,128)(2,1)} %param.21) | copy-start | bytes 786436
  101.0 13.5 %copy-start.3 = (bf16[2048,512]{1,0:T(8,128)(2,1)S(1)}, bf16[2048,512]{1,0:T(8,128)(2,1)}, u32[]{:S(2)}) copy-start(bf16[2048,512]{1,0:T(8,128)(2,1)} %param.16) | copy-start | bytes 6291460
  101.0 17.5 %copy-start.17 = (f32[512]{0:T(512)S(1)}, f32[512]{0:T(512)}, u32[]{:S(2)}) copy-start(f32[512]{0:T(512)} %param.24) | copy-start | bytes 6148
  101.0 17.5 %copy-start.21 = (f32[512]{0:T(512)S(1)}, f32[512]{0:T(512)}, u32[]{:S(2)}) copy-start(f32[512]{0:T(512)} %param.25) | copy-start | bytes 6148
  101.0 34.8 %all-gather.7.cloned.1.call-start = ((), (), s32[]{:S(2)}) async-start(), calls=%async_computation.6 | async-start | bytes 6291456 | tf_op jit(solution)/shard_map/all_gather | solution.py:135
  120.8 51.5 %reduce-scatter.7.cloned.1.call-start = ((), (), s32[]{:S(2)}) async-start(), calls=%async_computation.7 | async-start | bytes 6291456 | tf_op jit(solution)/shard_map/reduce_scatter | solution.py:138
  135.8 17.0 %copy-start.26 = (bf16[1024,512]{1,0:T(8,128)(2,1)S(1)}, bf16[1024,512]{1,0:T(8,128)(2,1)}, u32[]{:S(2)}) copy-start(bf16[1024,512]{1,0:T(8,128)(2,1)} %param.23) | copy-start | bytes 3145732
  158.8 40.9 %all-gather.9.cloned.1.call-start = ((), (), s32[]{:S(2)}) async-start(), calls=%async_computation.8 | async-start | bytes 6291456 | tf_op jit(solution)/shard_map/all_gather | solution.py:151
  184.7 54.9 %reduce-scatter.9.cloned.1.call-start = ((), (), s32[]{:S(2)}) async-start(), calls=%async_computation.9 | async-start | bytes 6291456 | tf_op jit(solution)/shard_map/reduce_scatter | solution.py:157
  226.1 13.5 %copy-start.8 = (f32[512,512]{1,0:T(8,128)S(1)}, f32[512,512]{1,0:T(8,128)}, u32[]{:S(2)}) copy-start(f32[512,512]{1,0:T(8,128)} %copy-done.6) | copy-start | bytes 3145732
  226.1 38.5 %all-gather.11.cloned.1.call-start = ((), (), s32[]{:S(2)}) async-start(), calls=%async_computation.10 | async-start | bytes 6291456 | tf_op jit(solution)/shard_map/all_gather | solution.py:168
  239.6 5.7 copy-start.5
  239.6 5.7 copy-start.9
  239.6 5.9 copy-start.11
  249.6 175.1 %reduce-scatter.11.cloned.1.call-start = ((), (), s32[]{:S(2)}) async-start(), calls=%async_computation.11 | async-start | bytes 6291456 | tf_op jit(solution)/shard_map/reduce_scatter | solution.py:182
  269.4 120.9 %copy-start.28 = (bf16[512,768]{1,0:T(8,128)(2,1)S(1)}, bf16[512,768]{1,0:T(8,128)(2,1)}, u32[]{:S(2)}) copy-start(bf16[512,768]{1,0:T(8,128)(2,1)} %param.20) | copy-start | bytes 2359300
  398.2 240.1 %all-reduce.7.cloned.1.call-start = ((), (), s32[]{:S(2)}) async-start(), calls=%async_computation.13 | async-start | bytes 12582912 | tf_op jit(solution)/shard_map/psum | solution.py:191
  398.5 10.6 %copy-start.24 = (bf16[4096,512]{1,0:T(8,128)(2,1)S(1)}, bf16[4096,512]{1,0:T(8,128)(2,1)}, u32[]{:S(2)}) copy-start(bf16[4096,512]{1,0:T(8,128)(2,1)} %all-gather.9.cloned.1.call-done) | copy-start | bytes 12582916
  398.5 21.4 %slice-start = ((s8[6291456]{0:T(1024)(128)(4,1)}), s8[4194304]{0:T(1024)(128)(4,1)S(1)}, s32[]{:S(2)}) async-start(s8[6291456]{0:T(1024)(128)(4,1)} %bitcast.186), calls=%async_computation.14 | async-start | bytes 8388608
  409.1 8.7 %copy-start.12 = (bf16[8,512,256]{2,1,0:T(8,128)(2,1)S(1)}, bf16[8,512,256]{2,1,0:T(8,128)(2,1)}, u32[]{:S(2)}) copy-start(bf16[8,512,256]{2,1,0:T(8,128)(2,1)} %get-tuple-element.71) | copy-start | bytes 6291460
  409.1 8.7 %copy-start.25 = (bf16[4096,512]{1,0:T(8,128)(2,1)S(1)}, bf16[4096,512]{1,0:T(8,128)(2,1)}, u32[]{:S(2)}) copy-start(bf16[4096,512]{1,0:T(8,128)(2,1)} %all-gather.11.cloned.1.call-done) | copy-start | bytes 12582916
  409.1 10.7 %slice-start.1 = ((s8[6291456]{0:T(1024)(128)(4,1)}), s8[2097152]{0:T(1024)(128)(4,1)S(1)}, s32[]{:S(2)}) async-start(s8[6291456]{0:T(1024)(128)(4,1)} %bitcast.186), calls=%async_computation.15 | async-start | bytes 4194304
  424.6 348.1 %all-reduce.5.cloned.1.call-start = ((), (), s32[]{:S(2)}) async-start(), calls=%async_computation.12 | async-start | bytes 2097152 | tf_op jit(solution)/shard_map/psum | solution.py:194
  431.1 4.3 copy-start.19
  431.1 4.3 copy-start.20
  638.3 140.4 %copy-start.14 = (f32[512,1024]{1,0:T(8,128)S(1)}, f32[512,1024]{1,0:T(8,128)}, u32[]{:S(2)}) copy-start(f32[512,1024]{1,0:T(8,128)} %get-tuple-element.277) | copy-start | bytes 6291460
  772.7 5.1 copy-start.15
  775.1 4.9 copy-start.13
  (18 other events, 56.4 us)
Sparse Core Ops, SparseCore 0:
  13.2 16.1 all-gather.4
  101.1 13.3 reduce-scatter.4
  120.9 14.8 all-gather.6
  158.9 13.3 reduce-scatter.6
  184.8 14.8 all-gather.8
  226.3 13.3 reduce-scatter.8
  249.7 14.8 all-gather.10
  398.3 13.3 reduce-scatter.10
  424.7 213.5 all-reduce.6
  643.9 128.7 all-reduce.4
where the time goes:
time: 799 us; the launch traced here: 789 us
  waiting for transfers between devices  395 us (49%)
  matrix products  186 us (23%)
  local copies, waits for them, and re-layouts  82.9 us (10%)
  other arithmetic  64.4 us (8%)
  blocking collectives  43.2 us (5%)
  between operations  14.9 us (2%)
    psum x1, waiting for transfers between devices, local(): lax.psum((qkv_grad, out_grad, up_grad, down_grad), 'dp')  160 us
    psum x1, waiting for transfers between devices, local(): lax.psum((pos_grad, gain_one_grad, bias_one_grad, gain_two_grad, bias_two...  134 us
    psum x1, blocking collectives, local(): lax.psum((pos_grad, gain_one_grad, bias_one_grad, gain_two_grad, bias_two...  43.2 us
    dot_general x4, matrix products, times_transposed(): lax.dot_general(left_side, right_side, (((1,), (1,)), ((), ())), preferre...  35.8 us
    dot_general x8, matrix products, attend_back(): jnp.einsum('qhd,khd->hqk', upstream, values, preferred_element_type=jnp.f...  30.9 us
    dynamic_slice x32, local copies, waits for them, and re-layouts, local(): lax.map(attend, (joined_piece.reshape(window_count, window_len, -1), segm...  30.7 us
    dot_general x16, matrix products, scores_of(): jnp.einsum('qhd,khd->hqk', queries, keys_in, preferred_element_type=jnp.f...  29.7 us
    dot_general x4, matrix products, cross_rows(): lax.dot_general(left_side, right_side, (((0,), (0,)), ((), ())), preferre...  25.9 us
  transfers between devices with their start and end apart: 10, of which 9 were waited for; matrix products, arithmetic and copies ran while one was open for 5% of the time, Pallas kernels for 0%

commit v1 on v0

v1 whole, which is shorter than its diff:
```python
import functools

import jax
import jax.numpy as jnp
from jax import lax
from jax.experimental import pallas as pl
from jax.experimental.pallas import tpu as pltpu
from jax.sharding import PartitionSpec as P

BF = jnp.bfloat16
F32 = jnp.float32
MESH = pl.DeviceIdType.MESH
HD = 64
EPSILON = 1e-05
NEG = -1e30
GELU_A = 0.7978845608028654
GELU_B = 0.044715

CHUNKS = {
    "D0": (32, 512),
    "D1": (32, 512),
    "U0": (32, 512),
    "U1": (32, 512),
    "O": (16, 512),
    "Q0": (32, 384),
    "Q1": (32, 384),
    "P": (16, 512),
}
NAMES = tuple(CHUNKS)
PIECES = 16

SCHEDULE = {
    ("down", 1): (("D0", 0),),
    ("down", 3): (("D1", 0),),
    ("slope", 1): (("D0", 1),),
    ("slope", 3): (("D1", 1),),
    ("up", 1): (("U0", 0),),
    ("up", 3): (("D0", 2), ("U1", 0),),
    ("nb", 0): (("U0", 1),),
    ("nb", 1): (("D1", 2), ("U1", 1),),
    ("nb", 2): (("D0", 3),),
    ("O", 0): (("O", 0), ("sm", 0),),
    ("back0", 0): (("U0", 2),),
    ("back0", 1): (("D1", 3),),
    ("back0", 2): (("D0", 4), ("U1", 2), ("O", 1), ("sm", 1),),
    ("back0", 4): (("U0", 3),),
    ("back0", 5): (("D1", 4),),
    ("back0", 6): (("U1", 3), ("sm", 2),),
    ("back0", 7): (("D0", 5), ("O", 2),),
    ("q0", 0): (("U0", 4),),
    ("q0", 1): (("Q0", 0),),
    ("back1", 0): (("D1", 5), ("sm", 3),),
    ("back1", 1): (("D0", 6), ("U1", 4),),
    ("back1", 2): (("O", 3), ("Q0", 1),),
    ("back1", 3): (("U0", 5), ("sm", 4),),
    ("back1", 4): (("D1", 6),),
    ("back1", 5): (("U1", 5),),
    ("back1", 6): (("D0", 7), ("O", 4),),
    ("back1", 7): (("Q0", 2),),
    ("q1", 0): (("U0", 6),),
    ("q1", 1): (("Q1", 0),),
    ("fin", 0): (("D1", 7), ("O", 5),),
    ("fin", 1): (("U1", 6),),
    ("fin", 2): (("Q0", 3),),
    ("P", 0): (("Q1", 1), ("P", 0),),
}
TAIL = (
    ("U0", 7),
    ("O", 6),
    ("P", 1),
    ("Q0", 4),
    ("U1", 7),
    ("Q1", 2),
    ("Q0", 5),
    ("O", 7),
    ("P", 2),
    ("Q1", 3),
    ("Q0", 6),
    ("P", 3),
    ("Q1", 4),
    ("P", 4),
    ("Q0", 7),
    ("Q1", 5),
    ("P", 5),
    ("Q1", 6),
    ("P", 6),
    ("Q1", 7),
    ("P", 7),
    ("P", 8),
)


def dot(left, right, left_dim=1, right_dim=0):
    return lax.dot_general(
        left, right, (((left_dim,), (right_dim,)), ((), ())), preferred_element_type=F32
    )


def lanes(shape):
    return lax.broadcasted_iota(jnp.int32, shape, len(shape) - 1)


def rows_of(w, win):
    return pl.ds(pl.multiple_of(w * win, win), win)


def columns_of(start, size):
    return pl.ds(pl.multiple_of(start, 128), size)


def row_mean(v):
    return jnp.mean(v, axis=-1, keepdims=True)


def kernel(fused, dims, *refs):
    win, width, hidden, windows = dims
    half_hidden = hidden // 2
    half = win // 2
    (tok_h, cot_h, pos_h, seg, wq_h, wo_h, wu_h, wd_h, g1, b1, g2, b2) = refs[:12]
    refs = refs[12:]
    out_h, ig_h, small_h = refs[:3]
    F = dict(zip(NAMES, refs[3 : 3 + len(NAMES)]))
    b = dict(zip(scratch_of(fused, dims), refs[3 + len(NAMES) :]))
    tok, cot, pos, augs, augk = b["tok"], b["cot"], b["pos"], b["augs"], b["augk"]
    wq, wo, wu, wd = b["wq"], b["wo"], b["wu"], b["wd"]
    joined, mix, u1, rs1, pb, nb = b["joined"], b["mix"], b["u1"], b["rs1"], b["pb"], b["nb"]
    act, gp, augq, nf, small = b["act"], b["gp"], b["augq"], b["nf"], b["small"]
    G, R_mp, R_a, R_b, R_z = ({k: b.get(buf + k) for k in NAMES} for buf in ("G", "M", "A", "B", "Z"))
    in_sem, out_sem = b["in_sem"], b["out_sem"]

    pairs = width // 128

    copies = {}

    def fetch(name, src, dst, k):
        copies[name] = pltpu.make_async_copy(src, dst, in_sem.at[k])
        copies[name].start()

    if fused:
        wsem, csend, crecv, ssend, srecv, lsem = (
            b[k] for k in ("wsem", "csend", "crecv", "ssend", "srecv", "lsem")
        )
        dp = lax.axis_index("dp")
        mp = lax.axis_index("mp")
        zc = dp // 4
        yc = lax.rem(dp // 2, 2)
        xc = lax.rem(dp, 2)
        ac = jnp.where(mp == 0, xc, yc)
        bc = jnp.where(mp == 0, yc, xc)
        step_a = jnp.where(mp == 0, 1, 2)
        step_b = jnp.where(mp == 0, 2, 1)
        dev_mp = (dp, 1 - mp)
        dev_a = (dp + step_a * (1 - 2 * ac), mp)
        dev_b = (dp + step_b * (1 - 2 * bc), mp)
        dev_x = (dp + 1 - 2 * xc, mp)
        dev_y = (dp + 2 * (1 - 2 * yc), mp)
        zs = [lax.rem(zc + k, 4) for k in (1, 2, 3)]
        dev_z = [(lax.rem(dp, 4) + 4 * z, mp) for z in zs]
        barrier = pltpu.get_barrier_semaphore()
        for dev in [dev_mp, dev_a, dev_b] + dev_z:
            pl.semaphore_signal(barrier, inc=1, device_id=dev, device_id_type=MESH)

    fetch("tok", tok_h, tok, 0)
    fetch("pos", pos_h, pos, 1)
    raw_width = wq_h.shape[1]
    raw = act.at[pl.ds(0, width), pl.ds(0, raw_width)]
    fetch("wq", wq_h, raw, 2)
    wparts = []
    if fused:
        wparts.append((wo_h, wo.at[pl.ds(pl.multiple_of(mp * half, half), half), :]))
        wparts.append((wu_h, wu.at[:, columns_of(half_hidden * mp, half_hidden)]))
        wparts.append((wd_h, wd.at[pl.ds(pl.multiple_of(mp * half_hidden, half_hidden), half_hidden), :]))
    else:
        wparts += [(wo_h, wo), (wu_h, wu), (wd_h, wd)]
    for i, (src, dst) in enumerate(wparts):
        fetch("w%d" % i, src, dst, 5 + i)
    fetch("cot", cot_h, cot, 4)
    small[...] = jnp.zeros_like(small)

    l64 = lax.rem(lanes((win, 128)), HD)
    lo = lanes((win, 128)) < HD

    copies["wq"].wait()
    own_columns = mp * raw_width // 3 if fused else 0
    for p in range(raw_width // 384):
        cut = [raw[:, pl.ds(p * 384 + 128 * i, 128)] for i in range(3)]
        low = lanes((width, 128)) < HD
        swapped = [pltpu.roll(c.astype(F32), HD, 1).astype(BF) for c in cut]
        q = jnp.where(low, cut[0], cut[1]) * BF(HD**-0.5)
        k = jnp.where(low, swapped[0], swapped[2])
        v = jnp.where(low, cut[1], cut[2])
        for i, part in enumerate((q, k, v)):
            wq[:, columns_of(own_columns + width * i + 128 * p, 128)] = part

    wremote = []
    if fused:
        pl.semaphore_wait(barrier, 6)
        slices = [wq.at[:, columns_of(own_columns + width * i, raw_width // 3)] for i in range(3)]
        for i, (src, dst) in enumerate([(x, x) for x in slices] + wparts):
            c = pltpu.make_async_remote_copy(
                src_ref=src, dst_ref=dst, send_sem=wsem.at[0, i], recv_sem=wsem.at[1, i],
                device_id=dev_mp, device_id_type=MESH,
            )
            c.start()
            wremote.append(c)

    columns = seg[...].astype(F32).T
    mine = (mp if fused else 0) * windows
    for w in range(windows):
        R = pl.ds(w * win, win)
        column = jnp.sum(
            jnp.where(lanes(columns.shape) == mine + w, columns, 0.0), axis=1, keepdims=True
        ).astype(jnp.int32)
        augs[R, :] = jnp.where((l64 < 8) & (l64 != column), NEG, 0.0).astype(BF)
        augk[R, :] = jnp.where((l64 == column) | ((l64 >= 8) & (l64 < 11)), 1.0, 0.0).astype(BF)

    def remote(src, dst, send, recv, dev):
        return pltpu.make_async_remote_copy(
            src_ref=src, dst_ref=dst, send_sem=send, recv_sem=recv, device_id=dev, device_id_type=MESH
        )

    def add(mine, got):
        mine[...] = mine[...] + got[...]

    def exchange(name, k):
        if not fused:
            return
        c = NAMES.index(name)
        g = G[name]
        own = g.at[mp]
        mp_copy = remote(g.at[1 - mp], R_mp[name], csend.at[c, 0], crecv.at[c, 0], dev_mp)
        a_copy = remote(own.at[pl.ds((1 - ac) * 8, 8)], R_a[name], csend.at[c, 1], crecv.at[c, 1], dev_a)
        b_copy = remote(own.at[pl.ds(ac * 8 + (1 - bc) * 4, 4)], R_b[name], csend.at[c, 2], crecv.at[c, 2], dev_b)
        base = ac * 8 + bc * 4
        z_copies = [
            remote(own.at[base + zs[j]], R_z[name].at[j], csend.at[c, 3 + j], crecv.at[c, 3 + j], dev_z[j])
            for j in range(3)
        ]
        full = g.at[1 - mp]
        done = F[name].at[mp] if name == "P" else F[name]
        put = pltpu.make_async_copy(full, done, lsem.at[c])
        zg_copies = [
            remote(full.at[base + zc], full.at[base + zc], csend.at[c, 6 + j], crecv.at[c, 6 + j], dev_z[j])
            for j in range(3)
        ]
        bg_copy = remote(full.at[pl.ds(base, 4)], full.at[pl.ds(base, 4)], csend.at[c, 9], crecv.at[c, 9], dev_b)
        ag_copy = remote(full.at[pl.ds(ac * 8, 8)], full.at[pl.ds(ac * 8, 8)], csend.at[c, 10], crecv.at[c, 10], dev_a)
        mg_copy = remote(full, b["XP"], csend.at[c, 11], crecv.at[c, 11], dev_mp)
        if k == 0:
            mp_copy.start()
        elif k == 1:
            mp_copy.wait()
            add(own, R_mp[name])
            a_copy.start()
        elif k == 2:
            a_copy.wait()
            add(own.at[pl.ds(ac * 8, 8)], R_a[name])
            b_copy.start()
        elif k == 3:
            b_copy.wait()
            add(own.at[pl.ds(base, 4)], R_b[name])
            for z in z_copies:
                z.start()
        elif k == 4:
            for z in z_copies:
                z.wait()
            total = own[base + zc].astype(F32)
            for j in range(3):
                total = total + R_z[name][j].astype(F32)
            if name in ("Q0", "Q1"):
                q, kk, v = total[:, :128] * (HD**-0.5), total[:, 128:256], total[:, 256:]
                total = jnp.concatenate(
                    [q[:, :HD], kk[:, :HD], v[:, :HD], q[:, HD:], kk[:, HD:], v[:, HD:]], axis=1
                )
            full[base + zc] = total.astype(BF)
            for z in zg_copies:
                z.start()
        elif k == 5:
            for z in zg_copies:
                z.wait()
            bg_copy.start()
        elif k == 6:
            bg_copy.wait()
            ag_copy.start()
        elif k == 7:
            ag_copy.wait()
            put.start()
            if name == "P":
                mg_copy.start()
        elif k == 8:
            mg_copy.wait()
            other = pltpu.make_async_copy(b["XP"], F[name].at[1 - mp], lsem.at[len(NAMES)])
            other.start()
            other.wait()
        elif k == 9:
            put.wait()

    def exchange_small(k):
        if not fused:
            return
        legs = [(b["s_mp"], dev_mp, 0), (b["s_x"], dev_x, 1), (b["s_y"], dev_y, 2)]
        if k > 0 and k <= 3:
            buf, dev, s = legs[k - 1]
            remote(small, buf, ssend.at[s], srecv.at[s], dev).wait()
            small[...] = small[...] + buf[...]
        if k < 3:
            buf, dev, s = legs[k]
            remote(small, buf, ssend.at[s], srecv.at[s], dev).start()
        zcs = [remote(small, b["s_z"].at[zc], ssend.at[3 + j], srecv.at[3 + j], dev_z[j]) for j in range(3)]
        if k == 3:
            b["s_z"][zc] = small[...]
            for z in zcs:
                z.start()
        if k == 4:
            for z in zcs:
                z.wait()
            small[...] = (b["s_z"][0] + b["s_z"][1]) + (b["s_z"][2] + b["s_z"][3])

    causal = jnp.where(lanes((half, half)) <= lax.broadcasted_iota(jnp.int32, (half, half), 0), 0.0, NEG)
    causal_t = jnp.where(lanes((half, half)) >= lax.broadcasted_iota(jnp.int32, (half, half), 0), 0.0, NEG)
    def attend(w, p):
        R = rows_of(w, win)
        Q, K, V = (joined[R, columns_of(width * i + p * 128, 128)] for i in range(3))
        aq, ak = augs[R, :], augk[R, :]
        ones = jnp.ones((win, 128), BF)
        zero = jnp.zeros((win, 128), BF)
        qs, ks, vs = [], [], []
        for h in range(2):
            mine = lo if h == 0 else ~lo
            qs.append(jnp.where(mine, Q, aq))
            ks.append(jnp.where(mine, K, ak))
            vs.append(jnp.concatenate([jnp.where(mine, V, zero), jnp.where(mine, ones, zero)], axis=1))
        for qb in range(2):
            kl = half * (qb + 1)
            es, ms = [], []
            for h in range(2):
                s = dot(qs[h][qb * half : (qb + 1) * half], ks[h][:kl], 1, 1)
                if qb == 0:
                    s = s + causal
                else:
                    s = jnp.concatenate([s[:, :half], s[:, half:] + causal], axis=1)
                m = jnp.max(s, axis=1, keepdims=True)
                es.append(jnp.exp(s - m).astype(BF))
                ms.append(m)
            ov = dot(jnp.concatenate(es, axis=1), jnp.concatenate([v[:kl] for v in vs], axis=0))
            total = ov[:, 128:]
            rr = pl.ds(pl.multiple_of(w * win + qb * half, half), half)
            mix[rr, columns_of(p * 128, 128)] = (ov[:, :128] / total).astype(BF)
            low = lo[:half]
            lse = jnp.where(low, ms[0], ms[1]) + jnp.log(total)
            x = -pltpu.roll(lse, HD, 1)
            hi = x.astype(BF)
            x = x - hi.astype(F32)
            mid = x.astype(BF)
            last = (x - mid.astype(F32)).astype(BF)
            l6 = l64[:half]
            a = aq[qb * half : (qb + 1) * half]
            a = jnp.where(l6 == 8, hi, a)
            a = jnp.where(l6 == 9, mid, a)
            augq[rr, columns_of(p * 128, 128)] = jnp.where(l6 == 10, last, a)

    copies["tok"].wait()
    copies["pos"].wait()
    for c in wremote[:3]:
        c.wait()

    def project(w, _):
        R = rows_of(w, win)
        row = (tok[R, :].astype(F32) + pos[...].astype(F32)).astype(BF)
        pb[R, :] = row
        for i in range(3):
            joined[R, pl.ds(width * i, width)] = dot(row, wq[:, pl.ds(width * i, width)]).astype(BF)
        return 0

    lax.fori_loop(0, windows, project, 0)

    def attend_window(w, _):
        for p in range(pairs):
            attend(w, p)
        return 0

    lax.fori_loop(0, windows, attend_window, 0)

    for i in range(3):
        copies["w%d" % i].wait()
    for c in wremote[3:]:
        c.wait()
    copies["cot"].wait()

    def feed(w, _):
        R = rows_of(w, win)
        r1 = (tok[R, :].astype(F32) + pos[...].astype(F32)) + dot(mix[R, :], wo[...])
        center = r1 - row_mean(r1)
        rstd = lax.rsqrt(row_mean(center * center) + EPSILON)
        unit = center * rstd
        u1[R, :] = unit.astype(BF)
        rs1[R, :] = jnp.broadcast_to(rstd, (win, 128))
        normed = unit * g1[...] + b1[...]
        nf[...] = normed
        nb[R, :] = normed.astype(BF)

        r2 = nf[...]
        for c in range(hidden // 512):
            cs = pl.ds(c * 512, 512)
            v = dot(nb[R, :], wu[:, cs]).astype(BF)
            v2 = v * v
            t = jnp.tanh(v * (BF(GELU_A) + BF(GELU_A * GELU_B) * v2))
            h = BF(0.5) + BF(0.5) * t
            active = v * h
            act[R, cs] = active
            gp[R, cs] = h + h * ((BF(1) - h) * (v * (BF(2 * GELU_A) + BF(6 * GELU_A * GELU_B) * v2)))
            r2 = r2 + dot(active, wd[cs, :])
        center = r2 - row_mean(r2)
        rstd = lax.rsqrt(row_mean(center * center) + EPSILON)
        unit = center * rstd
        tok[R, :] = (unit * g2[...] + b2[...]).astype(BF)
        up = cot[R, :].astype(F32)
        small[0:1, :] += jnp.sum(up * unit, axis=0, keepdims=True)
        small[1:2, :] += jnp.sum(up, axis=0, keepdims=True)
        e = up * g2[...]
        cot[R, :] = (rstd * (e - row_mean(e) - unit * row_mean(e * unit))).astype(BF)
        return 0

    lax.fori_loop(0, windows, feed, 0)
    out_copy = pltpu.make_async_copy(tok, out_h, out_sem.at[0])
    out_copy.start()

    def hooked(phase, body, count):
        def one(t, _):
            body(t, 0)
            for at in range(count):
                steps = SCHEDULE.get((phase, at))
                if steps:
                    pl.when(t == at)(functools.partial(run_steps, steps))
            return 0

        lax.fori_loop(0, count, one, 0)

    def run_steps(steps):
        for name, k in steps:
            if name == "sm":
                exchange_small(k)
            else:
                exchange(name, k)

    halves = hidden // 1024

    def down_tile(t, _):
        part, m = t // 2, lax.rem(t, 2)
        tile = m * halves + part
        d = dot(act[:, columns_of(tile * 512, 512)], cot[...], 0, 0).astype(BF).reshape(16, 32, 512)
        for i in range(2):

            @pl.when(part == i)
            def _():
                G["D%d" % i][m] = d

        return 0

    hooked("down", down_tile, hidden // 512)

    def slope(w, _):
        R = rows_of(w, win)
        for c in range(hidden // 512):
            cs = pl.ds(c * 512, 512)
            d = dot(cot[R, :], wd[pl.ds(c * 512, 512), :], 1, 1)
            gp[R, cs] = (d * gp[R, cs].astype(F32)).astype(BF)
        return 0

    hooked("slope", slope, windows)

    def up_tile(t, _):
        part, m = t // 2, lax.rem(t, 2)
        tile = m * halves + part
        d = dot(nb[...], gp[:, columns_of(tile * 512, 512)], 0, 0).astype(BF).reshape(16, 32, 512)
        for i in range(2):

            @pl.when(part == i)
            def _():
                G["U%d" % i][m] = d

        return 0

    hooked("up", up_tile, hidden // 512)

    def norm_back(w, _):
        R = rows_of(w, win)
        ng = cot[R, :].astype(F32) + dot(gp[R, :], wu[...], 1, 1)
        unit = u1[R, :].astype(F32)
        small[2:3, :] += jnp.sum(ng * unit, axis=0, keepdims=True)
        small[3:4, :] += jnp.sum(ng, axis=0, keepdims=True)
        e = ng * g1[...]
        rstd = rs1[R, 0:1]
        rg = (rstd * (e - row_mean(e) - unit * row_mean(e * unit))).astype(BF)
        cot[R, :] = rg
        u1[R, :] = dot(rg, wo[...], 1, 1).astype(BF)
        return 0

    hooked("nb", norm_back, windows)

    G["O"][...] = dot(mix[...], cot[...], 0, 0).astype(BF).reshape(2, 16, half // 16, 512)
    run_steps(SCHEDULE.get(("O", 0), ()))

    flip = (lax.broadcasted_iota(jnp.int32, (256, 128), 0) % 128 < HD) != (lanes((256, 128)) < HD)
    swap = jnp.where(flip, 1.0, 0.0).astype(BF)

    def attend_back(w, p):
        R = rows_of(w, win)
        pc = columns_of(p * 128, 128)
        Q, K, V = (joined[R, columns_of(width * i + p * 128, 128)] for i in range(3))
        D = u1[R, pc]
        prod = D.astype(F32) * mix[R, pc].astype(F32)
        ph = prod.astype(BF)
        pl_ = (prod - ph.astype(F32)).astype(BF)
        x = -dot(jnp.concatenate([ph, pl_], axis=1), swap)
        hi = x.astype(BF)
        mid = (x - hi.astype(F32)).astype(BF)
        zero = jnp.zeros((win, 128), BF)
        ad = jnp.where(l64 == 8, hi, jnp.where(l64 == 9, mid, zero))
        av = jnp.where((l64 == 8) | (l64 == 9), jnp.ones((win, 128), BF), zero)
        aq, ak = augq[R, pc], augk[R, :]
        dq, dk, dv = [None, None], [None, None], [None, None]

        def acc(to, i, v):
            to[i] = v if to[i] is None else to[i] + v

        for h in range(2):
            mine = lo if h == 0 else ~lo
            qa, ka, va, da = (jnp.where(mine, a, b) for a, b in ((Q, aq), (K, ak), (V, av), (D, ad)))
            qm, km, dm = (jnp.where(mine, a, zero) for a in (Q, K, D))
            for kb in range(2):
                q0 = kb * half
                ks = slice(kb * half, (kb + 1) * half)
                s = dot(ka[ks], qa[q0:], 1, 1)
                if kb == 1:
                    s = s + causal_t
                else:
                    s = jnp.concatenate([s[:, :half] + causal_t, s[:, half:]], axis=1)
                e = jnp.exp(s)
                pr = e.astype(BF)
                dpr = dot(va[ks], da[q0:], 1, 1)
                ds = (e * dpr).astype(BF)
                acc(dv, kb, dot(pr, dm[q0:]))
                acc(dk, kb, dot(ds, qm[q0:]))
                x = dot(ds, km[ks], 0, 0)
                if kb == 0:
                    acc(dq, 0, x[:half])
                    acc(dq, 1, x[half:])
                else:
                    acc(dq, 1, x)
        for i in range(2):
            rr = pl.ds(pl.multiple_of(w * win + i * half, half), half)
            for k, v in enumerate((dq, dk, dv)):
                joined[rr, columns_of(width * k + p * 128, 128)] = v[i].astype(BF)

    def back_group(group):
        def one(t, _):
            attend_back(lax.rem(t, windows), (t // windows) * 2 + group)
            return 0

        return one

    def qkv_grad(group):
        for m in range(2):
            p = 2 * m + group
            for i in range(3):
                d = dot(pb[...], joined[:, pl.ds(width * i + p * 128, 128)], 0, 0).astype(BF)
                G["Q%d" % group][m, :, :, pl.ds(128 * i, 128)] = d.reshape(16, 32, 128)
            run_steps(SCHEDULE.get(("q%d" % group, m), ()))

    hooked("back0", back_group(0), windows * pairs // 2)
    qkv_grad(0)
    hooked("back1", back_group(1), windows * pairs // 2)
    qkv_grad(1)

    def finish(w, _):
        R = rows_of(w, win)
        v = cot[R, :].astype(F32) + dot(joined[R, :], wq[...], 1, 1)
        nf[...] = jnp.where(w == 0, v, nf[...] + v)
        cot[R, :] = v.astype(BF)
        return 0

    hooked("fin", finish, windows)
    ig_copy = pltpu.make_async_copy(cot, ig_h, out_sem.at[1])
    ig_copy.start()
    G["P"][...] = nf[...].astype(BF).reshape(2, 16, half // 16, 512)
    small_copy = pltpu.make_async_copy(small, small_h, out_sem.at[2])
    small_copy.start()
    run_steps(SCHEDULE.get(("P", 0), ()))
    run_steps(TAIL)
    run_steps([(name, 9) for name in NAMES])
    if not fused:
        outs = [pltpu.make_async_copy(G[nm], F[nm], in_sem.at[i]) for i, nm in enumerate(NAMES)]
        for c in outs:
            c.start()
        for c in outs:
            c.wait()
    out_copy.wait()
    ig_copy.wait()
    small_copy.wait()


def scratch_of(fused, dims):
    win, width, hidden, windows = dims
    rows = win * windows
    V, dma = pltpu.VMEM, pltpu.SemaphoreType.DMA
    b = {k: V((rows, width), BF) for k in ("tok", "cot", "mix", "u1", "pb", "nb", "augq")}
    b.update({k: V((rows, hidden), BF) for k in ("act", "gp")})
    b.update(
        pos=V((win, width), BF),
        augs=V((rows, 128), BF),
        augk=V((rows, 128), BF),
        wq=V((width, 3 * width), BF),
        wo=V((width, width), BF),
        wu=V((width, hidden), BF),
        wd=V((hidden, width), BF),
        joined=V((rows, 3 * width), BF),
        rs1=V((rows, 128), F32),
        nf=V((win, width), F32),
        small=V((8, width), F32),
        in_sem=dma((12,)),
        out_sem=dma((3,)),
    )
    b.update({"G" + k: V((2, PIECES) + CHUNKS[k], BF) for k in NAMES})
    if fused:
        for buf, count in (("M", 16), ("A", 8), ("B", 4), ("Z", 3)):
            b.update({buf + k: V((count,) + CHUNKS[k], BF) for k in NAMES})
        b["XP"] = V((PIECES,) + CHUNKS["P"], BF)
        b.update({k: V((8, width), F32) for k in ("s_mp", "s_x", "s_y")})
        b.update(
            s_z=V((4, 8, width), F32),
            wsem=dma((2, 6)),
            csend=dma((len(NAMES), 12)),
            crecv=dma((len(NAMES), 12)),
            ssend=dma((6,)),
            srecv=dma((6,)),
            lsem=dma((len(NAMES) + 1,)),
        )
    return b


def layer(fused, tok, cot, pos, seg, wq, wo, wu, wd, g1, b1, g2, b2, hidden):
    rows, width = tok.shape
    win = pos.shape[0]
    windows = rows // win
    hbm = pl.BlockSpec(memory_space=pl.ANY)
    vmem = pl.BlockSpec(memory_space=pltpu.VMEM)
    shape = jax.ShapeDtypeStruct
    full = {k: (PIECES,) + v if fused and k != "P" else (2, PIECES) + v for k, v in CHUNKS.items()}
    outs = [shape((rows, width), BF), shape((rows, width), BF), shape((8, width), F32)]
    outs += [shape(full[k], BF) for k in NAMES]
    scratch = list(scratch_of(fused, (win, width, hidden, windows)).values())
    params = dict(vmem_limit_bytes=64 << 20)
    if fused:
        params.update(collective_id=0, has_side_effects=True)
    return pl.pallas_call(
        functools.partial(kernel, fused, (win, width, hidden, windows)),
        out_shape=outs,
        in_specs=[hbm] * 3 + [vmem] + [hbm] * 4 + [vmem] * 4,
        out_specs=[hbm] * len(outs),
        scratch_shapes=scratch,
        compiler_params=pltpu.CompilerParams(**params),
        name="layer",
    )(tok, cot, pos, seg, wq, wo, wu, wd, g1, b1, g2, b2)


def finish_kernel(*refs):
    (out_h, ig_h, small), grads = refs[:3], dict(zip(NAMES, refs[3 : 3 + len(NAMES)]))
    refs = refs[3 + len(NAMES) :]
    out_o, ig_o, pos_o, qkv_o, wo_o, up_o, down_o = refs[:7]
    norms = refs[7:11]
    refs = refs[11:]
    got = dict(zip(NAMES, refs[: len(NAMES)]))
    wide = dict(zip(NAMES, refs[len(NAMES) : 2 * len(NAMES)]))
    held, in_sem, out_sem = refs[2 * len(NAMES) :]
    last, loads, passed = [], [], []
    for i, (src, dst) in enumerate(((out_h, out_o), (ig_h, ig_o))):
        passed.append(pltpu.make_async_copy(src, held.at[i], in_sem.at[len(NAMES) + i]))
        last.append(pltpu.make_async_copy(held.at[i], dst, out_sem.at[len(NAMES) + i]))
    for c in passed:
        c.start()
    for i, k in enumerate(NAMES):
        loads.append(pltpu.make_async_copy(grads[k], got[k], in_sem.at[i]))
        loads[-1].start()
    rows = down_o.shape[0] // 2
    places = {
        "D0": down_o.at[pl.ds(0, rows)],
        "D1": down_o.at[pl.ds(rows, rows)],
        "U0": up_o.at[:, pl.ds(0, 512)],
        "U1": up_o.at[:, pl.ds(512, 512)],
        "O": wo_o,
        "Q0": qkv_o.at[:, pl.ds(0, 384)],
        "Q1": qkv_o.at[:, pl.ds(384, 384)],
        "P": pos_o,
    }
    for i in range(2):
        passed[i].wait()
        last[i].start()
    for i, k in enumerate(NAMES):
        loads[i].wait()
        wide[k][...] = got[k][...].astype(F32).reshape(wide[k].shape)
        last.append(pltpu.make_async_copy(wide[k], places[k], out_sem.at[i]))
        last[-1].start()
    for ref, row in zip(norms, (2, 3, 0, 1)):
        ref[...] = small[row]
    for c in last:
        c.wait()


def finish(out, ig, small, grads, win, width, hidden):
    hbm = pl.BlockSpec(memory_space=pl.ANY)
    vmem = pl.BlockSpec(memory_space=pltpu.VMEM)
    shape = jax.ShapeDtypeStruct
    outs = [shape(out.shape, BF), shape(ig.shape, BF), shape((win, width), F32)]
    outs += [shape((width, 3 * width // 2), F32), shape((width // 2, width), F32)]
    outs += [shape((width, hidden // 2), F32), shape((hidden // 2, width), F32)]
    outs += [shape((width,), F32)] * 4
    dma = pltpu.SemaphoreType.DMA
    scratch = [pltpu.VMEM(g.shape, BF) for g in grads]
    scratch += [pltpu.VMEM((g.size // g.shape[-1], g.shape[-1]), F32) for g in grads]
    scratch += [pltpu.VMEM((2,) + out.shape, BF), dma((len(NAMES) + 2,)), dma((len(NAMES) + 2,))]
    return pl.pallas_call(
        finish_kernel,
        out_shape=outs,
        in_specs=[hbm, hbm, vmem] + [hbm] * len(NAMES),
        out_specs=[hbm] * 7 + [vmem] * 4,
        scratch_shapes=scratch,
        compiler_params=pltpu.CompilerParams(vmem_limit_bytes=64 << 20),
        name="finish",
    )(out, ig, small, *grads)


def local(shards, tokens, segment_ids, cotangent, pos_table, w_qkv, w_out, w_up, w_down, g1, b1, g2, b2):
    dp_size, mp_size = shards
    width = tokens.shape[1]
    win = pos_table.shape[0]
    hidden = w_up.shape[1] * mp_size
    fused = dp_size == PIECES
    gains = [v.reshape(1, width) for v in (g1, b1, g2, b2)]
    if fused:
        out, ig, small, *grads = layer(
            True, tokens, cotangent, pos_table, segment_ids, w_qkv, w_out, w_up, w_down, *gains, hidden
        )
        return tuple(finish(out, ig, small, grads, win, width, hidden))
    windows = tokens.shape[0] // win
    seg = jnp.roll(segment_ids, -lax.axis_index("mp") * windows, axis=0)
    wq = lax.all_gather(w_qkv, "mp", axis=1, tiled=True)
    wo = lax.all_gather(w_out, "mp", axis=0, tiled=True)
    wu = lax.all_gather(w_up, "mp", axis=1, tiled=True)
    wd = lax.all_gather(w_down, "mp", axis=0, tiled=True)
    out, ig, small, *grads = layer(False, tokens, cotangent, pos_table, seg, wq, wo, wu, wd, *gains, hidden)
    g = dict(zip(NAMES, (v.astype(F32) for v in grads)))
    g = {
        k: v if k == "P" else lax.psum(lax.psum_scatter(v, "mp", scatter_dimension=0, tiled=False), "dp")
        for k, v in g.items()
    }
    pos, small = lax.psum((g["P"], small), ("dp", "mp"))
    scale = jnp.array([HD**-0.5, 1, 1], F32)[:, None, None]
    Q = [(g[k].reshape(width, 3, 2, HD) * scale).transpose(0, 2, 1, 3).reshape(width, 6 * HD) for k in ("Q0", "Q1")]
    return (
        out,
        ig,
        pos.reshape(win, width),
        jnp.concatenate(Q, axis=1),
        g["O"].reshape(-1, width),
        jnp.concatenate([g["U0"].reshape(width, -1), g["U1"].reshape(width, -1)], axis=1),
        jnp.concatenate([g["D0"].reshape(-1, width), g["D1"].reshape(-1, width)], axis=0),
        small[2],
        small[3],
        small[0],
        small[1],
    )


def solution(mesh):
    cut, copied = P(("dp", "mp"), None), P()
    columns, split_rows = P(None, "mp"), P("mp", None)
    weights = (columns, split_rows, columns, split_rows)
    return jax.shard_map(
        functools.partial(local, (mesh.shape["dp"], mesh.shape["mp"])),
        mesh=mesh,
        in_specs=(cut, P("dp", None), cut, copied) + weights + (copied,) * 4,
        out_specs=(cut, cut, copied) + weights + (copied,) * 4,
        check_vma=False,
    )
```

time: 799 us -> 149 us (0.19); the launches traced: 789 us -> 148 us
  waiting for transfers between devices: 395 us -> 0 us
  matrix products: 186 us -> 0 us
  Pallas kernels: 0 us -> 148 us
  local copies, waits for them, and re-layouts: 82.9 us -> 0 us
  other arithmetic: 64.4 us -> 0 us
  blocking collectives: 43.2 us -> 0 us
  between operations: 14.9 us -> 0.84 us
    psum x2 -> x0, waiting for transfers between devices: 294 us -> none  [the longest x1 160 us: local(): lax.psum((qkv_grad, out_grad, up_grad, down_grad), 'dp')]
    dot_general x68 -> x0, matrix products: 186 us -> none  [the longest x4 35.8 us: times_transposed(): lax.dot_general(left_side, right_side, (((1,), (1,)), ((), ())), preferre...]
    pallas_call x0 -> x2, Pallas kernels: none -> 148 us  [the longest x1 140 us: layer(): pl.pallas_call(functools.partial(kernel, fused, (win, width, hidden, wind...]
    all_gather x4 -> x0, waiting for transfers between devices: 61.1 us -> none  [the longest x1 16.2 us: local(): shard_piece = lax.all_gather(mixed_in, 'mp', axis=0, tiled=True)]
    psum x1 -> x0, blocking collectives: 43.2 us -> none  [local(): lax.psum((pos_grad, gain_one_grad, bias_one_grad, gain_two_grad, bias_two...]
    dynamic_slice x48 -> x0, local copies, waits for them, and re-layouts: 39.6 us -> none  [the longest x32 30.7 us: local(): lax.map(attend, (joined_piece.reshape(window_count, window_len, -1), segm...]
    reduce_scatter x4 -> x0, waiting for transfers between devices: 39.5 us -> none  [the longest x1 13.3 us: local(): lax.psum_scatter(jnp.dot(active_piece, w_down, preferred_element_type=jnp...]
    convert_element_type x14 -> x0, other arithmetic: 31.7 us -> none  [the longest x8 10 us: attend_back(): score_grad = (probabilities * (prob_grad - centre)).astype(jnp.bfloat16)]
  transfers between devices with their start and end apart: 10 -> 0, of which waited for: 9 -> 0; matrix products, arithmetic and copies ran while one was open for 5% -> 0% of each run, Pallas kernels for 0% -> 0%
where the time goes in v1:
time: 149 us; the launch traced here: 148 us
  Pallas kernels  148 us (99%)
    pallas_call x1, Pallas kernels, layer(): pl.pallas_call(functools.partial(kernel, fused, (win, width, hidden, wind...  140 us
    pallas_call x1, Pallas kernels, finish(): pl.pallas_call(finish_kernel, out_shape=outs, in_specs=[hbm, hbm, vmem] +...  7.57 us

profile of v1, /device:TPU:1, one launch (start us, length us, event | category | flops | bytes accessed | tf_op | source)
XLA Modules:
  0.0 148.3 jit_solution(11425027981652284065)
XLA Ops:
  0.6 139.9 %layer.1 = (bf16[2048,512]{1,0:T(8,128)(2,1)}, bf16[2048,512]{1,0:T(8,128)(2,1)}, f32[8,512]{1,0:T(8,128)}, bf16[16,32,512]{2,1,0:T(8,128)(2,1)}, bf16[16,32,512...) custom-call(bf16[2048,512]{1,0:T(8,128)(2,1)} %refs_0_.1, ...), custom_call_target="tpu_custom_call" | custom-call | tf_op jit(solution)/shard_map/layer/pallas_call | solution.py:656
  140.6 7.6 %finish.1 = (bf16[2048,512]{1,0:T(8,128)(2,1)}, bf16[2048,512]{1,0:T(8,128)(2,1)}, f32[512,512]{1,0:T(8,128)}, f32[512,768]{1,0:T(8,128)}, f32[256,512]{1,0:T(8,...) custom-call(bf16[2048,512]{1,0:T(8,128)(2,1)} %get-tuple-element.22., ...), custom_call_target="tpu_custom_call" | custom-call | tf_op jit(solution)/shard_map/finish/pallas_call | solution.py:722
